TPU v7x, 512 devices: a whole 4x8x8 slice. The times are simulated.
512 devices in a mesh: rec: 16 (over z, core), frame: 32 (over x, y).
Axes of the slice: x: 4, y: 8, z: 8, core: 2. Of those that a mesh axis runs over, the one named last changes fastest.
Arguments:
- frames: bfloat16 [16, 49152, 256], P('rec', 'frame'), may hold values from -10 to 10
- texts: bfloat16 [32, 224, 256], P('rec', 'frame'), may hold values from -100 to 100
- pair_rec: int32 [32, 1], replicated, may hold values from 0 to 15, as said below
- pair_text: int32 [32], replicated, may hold values from 0 to 31, as said below
- pair_label: int32 [32], replicated, may hold values 0 or 1
Outputs:
- loss: float32 [], replicated
- grad_frames: bfloat16 [16, 49152, 256], P('rec', 'frame')
- grad_texts: bfloat16 [32, 224, 256], P('rec', 'frame')
Inputs may be any that keep to these rules, and one draw needn't show every extreme that they name: `pair_rec`: no recording is named by more than 6 pairs, some recording by exactly 6, and every recording by at least one. A pair's text is held by the index of rec one after, one before, or 8 after its recording (counted round): pair_text // 2 = (pair_rec + k) mod 16 with k one of 1, 15, 8.
All inputs are finite; a program needn't handle non-finite values.
Results may differ from a plain program's by a relative error of at most 0.0085.
Values may be sent and summed in bfloat16 or wider, within the bound.
A program may use at most 64 MiB of HBM per device.

v0:
```python
import jax
import jax.numpy as jnp
from jax import lax
from jax.sharding import PartitionSpec as P

MOST = 6
EPS = 1e-06
TEMP = 10.0
BIAS = -1.0
LOSS_SCALE = 2048.0


def slot_tables(pair_rec, pair_text, pair_label, here, most):
    record = pair_rec[:, 0]
    count = record.shape[0]
    order = jnp.arange(count, dtype=jnp.int32)
    same = (record[:, None] == record[None, :]).astype(jnp.int32)
    earlier = (order[None, :] < order[:, None]).astype(jnp.int32)
    rank = jnp.sum(same * earlier, axis=1)
    places = jnp.arange(most, dtype=jnp.int32)
    chosen = ((record[None, :] == here) & (rank[None, :] == places[:, None])).astype(jnp.int32)
    valid = jnp.sum(chosen, axis=1)
    slot_text = jnp.sum(chosen * pair_text[None, :], axis=1)
    sign = jnp.sum(chosen * (2 * pair_label[None, :] - 1), axis=1)
    return (valid, slot_text, sign)


def pair_terms(score, valid, sign, tokens):
    margin = -sign * (TEMP * score + BIAS)
    loss_part = valid * jax.nn.softplus(margin)
    grad_cos = -LOSS_SCALE * TEMP * valid * sign * jax.nn.sigmoid(margin) / tokens
    return (loss_part, grad_cos)


def body(frames, texts, pair_rec, pair_text, pair_label):
    here = lax.axis_index("rec")
    part = lax.axis_index("frame")
    owned, width_rows, width = texts.shape
    tokens = width_rows * lax.axis_size("frame")
    n_text = owned * lax.axis_size("rec")
    valid, slot_text, sign = slot_tables(pair_rec, pair_text, pair_label, here, MOST)
    valid_f = valid.astype(jnp.float32)
    sign_f = sign.astype(jnp.float32)
    picks = (
        (slot_text[:, None] == jnp.arange(n_text, dtype=jnp.int32)[None, :]) & (valid[:, None] > 0)
    ).astype(jnp.bfloat16)
    whole = lax.all_gather(texts, "frame", axis=1, tiled=True)
    query_vectors = jnp.einsum(
        "jc,cgx->jgx",
        picks,
        lax.all_gather(whole, "rec", axis=0, tiled=True),
        preferred_element_type=jnp.float32,
    ).astype(jnp.bfloat16)
    upstream_signal = frames[0]
    logit_scale = width ** (-0.5)
    pair_scores = (
        jnp.einsum(
            "ype,je->ypj", query_vectors, upstream_signal, preferred_element_type=jnp.float32
        )
        * logit_scale
    )
    local_max = jnp.max(pair_scores, axis=2)
    row_max = lax.pmax(local_max, "frame")
    expo = jnp.exp(pair_scores - row_max[..., None])
    batch_weights = expo.astype(jnp.bfloat16)
    value_partial = jnp.einsum(
        "pqx,xh->pqh", batch_weights, upstream_signal, preferred_element_type=jnp.float32
    )
    query_f = query_vectors.astype(jnp.float32)
    q_norm = lax.rsqrt(jnp.sum(query_f * query_f, axis=2) + EPS)
    q_unit = query_f * q_norm[..., None]
    context = lax.psum(value_partial, "frame")
    c_norm = lax.rsqrt(jnp.sum(context * context, axis=2) + EPS)
    c_unit = context * c_norm[..., None]
    cos = jnp.sum(q_unit * c_unit, axis=2)
    score = jnp.mean(cos, axis=1)
    loss_part, grad_cos = pair_terms(score, valid_f, sign_f, tokens)
    weight = grad_cos[:, None, None]
    d_context = weight * (q_unit - cos[..., None] * c_unit) * c_norm[..., None]
    direct = weight * (c_unit - cos[..., None] * q_unit) * q_norm[..., None]
    direct_own = lax.dynamic_slice_in_dim(direct, part * width_rows, width_rows, 1)
    context_batch_gradient = d_context.astype(jnp.bfloat16)
    weight_gradient = jnp.einsum(
        "ype,je->ypj", context_batch_gradient, upstream_signal, preferred_element_type=jnp.float32
    )
    score_gradient = (expo * weight_gradient * logit_scale).astype(jnp.bfloat16)
    d_query = lax.psum_scatter(
        jnp.einsum(
            "slf,fd->lsd", score_gradient, upstream_signal, preferred_element_type=jnp.float32
        ),
        "frame",
        scatter_dimension=0,
        tiled=True,
    )
    d_query = d_query + jnp.transpose(direct_own, (1, 0, 2))
    text_term = jnp.einsum(
        "st,lsd->tld", picks.astype(jnp.float32), d_query, precision=lax.Precision.HIGHEST
    )
    grad_texts = lax.psum_scatter(text_term, "rec", scatter_dimension=0, tiled=True).astype(
        jnp.bfloat16
    )
    frame_loss_piece = jnp.einsum(
        "cvm,cvz->mz", score_gradient, query_vectors, preferred_element_type=jnp.float32
    )
    frame_loss_piece = frame_loss_piece + jnp.einsum(
        "cvm,cvz->mz", batch_weights, context_batch_gradient, preferred_element_type=jnp.float32
    )
    grad_frames = frame_loss_piece.astype(jnp.bfloat16)[None]
    loss = lax.psum(jnp.sum(loss_part), "rec")
    return (loss, grad_frames, grad_texts)


def solution(mesh):
    return jax.shard_map(
        body,
        mesh=mesh,
        in_specs=(P("rec", "frame", None), P("rec", "frame", None), P(), P(), P()),
        out_specs=(P(), P("rec", "frame", None), P("rec", "frame", None)),
        check_vma=False,
    )
```

profile of v0, /device:TPU:16, one launch (start us, length us, event | category | flops | bytes accessed | tf_op | source)
XLA Modules:
  0.0 644.4 jit_solution(15901261809968272552)
XLA Ops:
  7.2 49.8 %all_gather.6 = bf16[2,224,256]{2,0,1:T(2,128)(2,1)S(1)} all-gather(bf16[2,7,256]{2,0,1:T(2,128)(2,1)} %param.6), channel_id=1, replica_groups=mesh['rec'=16,'frame'=32] {'frame'}, dimensions={1}, use_global_device_ids=true | all-gather | bytes 236544 | tf_op jit(solution)/shard_map/all_gather | solution.py:47
  57.0 0.7 copy.20
  57.8 0.9 select_reduce_fusion
  60.1 1.3 select_reduce_fusion.2
  61.4 43.4 %all-gather.2.cloned.1.call-done = bf16[32,224,256]{2,1,0:T(8,128)(2,1)} async-done(((bf16[2,224,256]{2,1,0:T(8,128)(2,1)}), bf16[32,224,256]{2,1,0:T(8,128)(2,1)}) %all-gather.2.cloned.1.call-update) | async-done | bytes 3670032 | tf_op jit(solution)/shard_map/all_gather | solution.py:51
  104.7 4.3 fusion.6
  109.0 4.4 multiply_reduce_fusion
  113.4 71.4 %pmax.7 = f32[6,224]{1,0:T(8,128)S(1)} all-reduce(f32[6,224]{1,0:T(8,128)S(1)} %get-tuple-element.17), channel_id=1, replica_groups=mesh['rec'=16,'frame'=32] {'frame'}, use_global_device_ids=true, to_apply=%region_6.0 | all-reduce | flops 1344 | bytes 10752 | tf_op jit(solution)/shard_map/pmax | solution.py:63
  184.8 4.9 fusion.13
  189.7 2.1 copy.23
  192.6 157.1 %all-reduce.5.cloned.1.call-done = f32[6,224,256]{2,0,1:T(8,128)} async-done(((f32[6,224,256]{2,0,1:T(8,128)}), f32[6,224,256]{2,0,1:T(8,128)}) %all-reduce.5.cloned.1.call-update) | async-done | bytes 1376272 | tf_op jit(solution)/shard_map/psum | solution.py:72
  349.7 1.9 multiply_reduce_fusion.1
  351.6 2.4 multiply_reduce_fusion.2
  354.0 1.4 fusion.44
  355.4 1.8 convert_multiply_fusion
  357.2 4.9 multiply_convert_fusion
  362.2 1.3 fusion.10
  364.2 2.1 copy.47
  366.2 1.3 dynamic-slice
  369.6 5.7 convolution_bitcast_fusion
  375.3 2.3 fusion.5
  377.6 209.2 %reduce-scatter.3.cloned.1.call-done = f32[7,6,256]{2,1,0:T(8,128)} async-done(((f32[224,6,256]{2,1,0:T(8,128)}), f32[7,6,256]{2,1,0:T(8,128)}) %reduce-scatter.3.cloned.1.call-update) | async-done | bytes 43024 | tf_op jit(solution)/shard_map/reduce_scatter | solution.py:87
  586.9 1.3 fusion.27
  588.2 49.1 %all-reduce.6 = (f32[]{:T(128)}, bf16[32,7,256]{2,0,1:T(8,128)(2,1)S(1)}) all-reduce(f32[]{:T(128)} %get-tuple-element.14, f32[32,7,256]{2,0,1:T(8,128)S(1)} %fusion.27), channel_id=1, replica_groups=mesh['rec'=16,'frame'=32] {'rec'}, use_global_device_ids=true, to_apply=%region_11.12 | all-reduce | flops 57345 | bytes 344072 | tf_op jit(solution)/shard_map/psum | solution.py:109
  (38 shorter events, 5.2 us)
Async XLA Ops:
  7.2 101.8 %copy-start = (bf16[1,1536,256]{2,1,0:T(8,128)(2,1)S(1)}, bf16[1,1536,256]{2,1,0:T(8,128)(2,1)}, u32[]{:S(2)}) copy-start(bf16[1,1536,256]{2,1,0:T(8,128)(2,1)} %param.5) | copy-start | bytes 2359300
  7.2 97.5 %all-gather.2.cloned.1.call-start = ((), (), s32[]{:S(2)}) async-start(), calls=%async_computation.1 | async-start | bytes 3899392 | tf_op jit(solution)/shard_map/all_gather | solution.py:51
  57.8 291.9 %all-reduce.5.cloned.1.call-start = ((), (), s32[]{:S(2)}) async-start(), calls=%async_computation.2 | async-start | bytes 3670016 | tf_op jit(solution)/shard_map/psum | solution.py:72
  61.3 43.4 %copy-start.9 = (s32[6]{0:T(128)}, s32[6]{0:T(128)S(1)}, u32[]{:S(2)}) copy-start(s32[6]{0:T(128)S(1)} %get-tuple-element.7) | copy-start | bytes 76
  61.3 47.6 %copy-start.4 = (s32[6]{0:T(128)}, s32[6]{0:T(128)S(1)}, u32[]{:S(2)}) copy-start(s32[6]{0:T(128)S(1)} %get-tuple-element.6) | copy-start | bytes 76
  61.4 47.6 %copy-start.8 = (pred[6]{0:T(512)(128)(4,1)}, pred[6]{0:T(512)(128)(4,1)S(1)}, u32[]{:S(2)}) copy-start(pred[6]{0:T(512)(128)(4,1)S(1)} %broadcast_compare_fusion) | copy-start | bytes 22
  191.8 395.1 %reduce-scatter.3.cloned.1.call-start = ((), (), s32[]{:S(2)}) async-start(), calls=%async_computation.3 | async-start | bytes 1892352 | tf_op jit(solution)/shard_map/reduce_scatter | solution.py:87
  349.7 5.7 copy-start.1
  354.0 3.2 copy-start.3
  355.4 6.8 %copy-start.6 = (f32[6]{0:T(128)}, f32[6]{0:T(128)S(1)}, u32[]{:S(2)}) copy-start(f32[6]{0:T(128)S(1)} %get-tuple-element.13) | copy-start | bytes 76
  357.2 5.0 copy-start.2
  362.2 2.0 copy-start.10
  369.6 5.7 copy-start.11
  375.3 211.6 %copy-start.5 = (s32[6]{0:T(128)S(1)}, s32[6]{0:T(128)}, u32[]{:S(2)}) copy-start(s32[6]{0:T(128)} %copy-done.4) | copy-start | bytes 76
  375.3 211.6 %copy-start.7 = (f32[6]{0:T(128)S(1)}, f32[6]{0:T(128)}, u32[]{:S(2)}) copy-start(f32[6]{0:T(128)} %copy-done.6) | copy-start | bytes 76
Sparse Core Ops, SparseCore 0:
  57.9 46.7 all-gather.1
  191.9 157.7 all-reduce.4
  366.4 220.4 reduce-scatter.2
where the time goes:
time: 645 us; the launch traced here: 644 us
  waiting for transfers between devices  410 us (64%)
  blocking collectives  170 us (26%)
  matrix products  29 us (4%)
  between operations  14.6 us (2%)
  other arithmetic  11.7 us (2%)
  local copies, waits for them, and re-layouts  8.88 us (1%)
    reduce_scatter x1, waiting for transfers between devices, body(): lax.psum_scatter(jnp.einsum('slf,fd->lsd', score_gradient, upstream_signa...  209 us
    psum x1, waiting for transfers between devices, body(): context = lax.psum(value_partial, 'frame')  157 us
    pmax x1, blocking collectives, body(): row_max = lax.pmax(local_max, 'frame')  71.4 us
    all_gather x1, blocking collectives, body(): whole = lax.all_gather(texts, 'frame', axis=1, tiled=True)  49.8 us
    psum x1, blocking collectives, body(): loss = lax.psum(jnp.sum(loss_part), 'rec')  49.1 us
    all_gather x1, waiting for transfers between devices, body(): lax.all_gather(whole, 'rec', axis=0, tiled=True)  43.4 us
  transfers between devices with their start and end apart: 3, of which 3 were waited for; matrix products, arithmetic and copies ran while one was open for 2% of the time, Pallas kernels for 0%

commit v1 on v0

--- a/solution.py
+++ b/solution.py
@@ -69,7 +69,9 @@
     query_f = query_vectors.astype(jnp.float32)
     q_norm = lax.rsqrt(jnp.sum(query_f * query_f, axis=2) + EPS)
     q_unit = query_f * q_norm[..., None]
-    context = lax.psum(value_partial, "frame")
+    context = value_partial
+    for hop in (1, 2, 4, 8, 16):
+        context = context + lax.ppermute(context, "frame", [(dev, dev ^ hop) for dev in range(32)])
     c_norm = lax.rsqrt(jnp.sum(context * context, axis=2) + EPS)
     c_unit = context * c_norm[..., None]
     cos = jnp.sum(q_unit * c_unit, axis=2)

time: 645 us -> 614 us (0.952)
  waiting for transfers between devices: 410 us -> 368 us
  starting transfers between devices: 0.3 us -> 18.4 us
    reduce_scatter x1 -> x0, waiting for transfers between devices: 209 us -> none  [body(): lax.psum_scatter(jnp.einsum('slf,fd->lsd', score_gradient, upstream_signa...]
    unnamed x3, waiting for transfers between devices: 0.05 us -> 166 us
    ppermute x0 -> x5, waiting for transfers between devices: none -> 158 us  [body(): lax.ppermute(context, 'frame', [(dev, dev ^ hop) for dev in range(32)])]
    psum x1 -> x0, waiting for transfers between devices: 157 us -> none  [body(): context = lax.psum(value_partial, 'frame')]
    ppermute x0 -> x5, starting transfers between devices: none -> 18.4 us  [body(): lax.ppermute(context, 'frame', [(dev, dev ^ hop) for dev in range(32)])]
  transfers between devices with their start and end apart: 3 -> 7, of which waited for: 3 -> 7; matrix products, arithmetic and copies ran while one was open for 2% -> 2% of each run, Pallas kernels for 0% -> 0%
where the time goes in v1:
time: 614 us
  waiting for transfers between devices  368 us (60%)
  blocking collectives  170 us (28%)
  matrix products  26.3 us (4%)
  starting transfers between devices  18.4 us (3%)
  between operations  15.5 us (3%)
  other arithmetic  8.49 us (1%)
  local copies, waits for them, and re-layouts  6.54 us (1%)
    unnamed x3, waiting for transfers between devices  166 us
    ppermute x5, waiting for transfers between devices, body(): lax.ppermute(context, 'frame', [(dev, dev ^ hop) for dev in range(32)])  158 us
    pmax x1, blocking collectives, body(): row_max = lax.pmax(local_max, 'frame')  71.3 us
    all_gather x1, blocking collectives, body(): whole = lax.all_gather(texts, 'frame', axis=1, tiled=True)  49.8 us
    psum x1, blocking collectives, body(): loss = lax.psum(jnp.sum(loss_part), 'rec')  49.1 us
    all_gather x1, waiting for transfers between devices, body(): lax.all_gather(whole, 'rec', axis=0, tiled=True)  43.8 us
    ppermute x5, starting transfers between devices, body(): lax.ppermute(context, 'frame', [(dev, dev ^ hop) for dev in range(32)])  18.4 us
  transfers between devices with their start and end apart: 7, of which 7 were waited for; matrix products, arithmetic and copies ran while one was open for 2% of the time, Pallas kernels for 0%

profile of v1, /device:TPU:16, one launch (start us, length us, event | category | flops | bytes accessed | tf_op | source)
XLA Modules:
  0.0 613.8 jit_solution(13758705461403345661)
XLA Ops:
  7.2 49.8 %all_gather.6 = bf16[2,224,256]{2,0,1:T(2,128)(2,1)S(1)} all-gather(bf16[2,7,256]{2,0,1:T(2,128)(2,1)} %param.6), channel_id=1, replica_groups=mesh['rec'=16,'frame'=32] {'frame'}, dimensions={1}, use_global_device_ids=true | all-gather | bytes 236544 | tf_op jit(solution)/shard_map/all_gather | solution.py:47
  60.9 43.8 %all-gather.2.cloned.1.call-done = bf16[32,224,256]{2,1,0:T(8,128)(2,1)} async-done(((bf16[2,224,256]{2,1,0:T(8,128)(2,1)}), bf16[32,224,256]{2,1,0:T(8,128)(2,1)}) %all-gather.2.cloned.1.call-update) | async-done | bytes 3670032 | tf_op jit(solution)/shard_map/all_gather | solution.py:51
  104.7 4.1 fusion.1
  109.2 4.4 multiply_reduce_fusion
  113.6 71.3 %pmax.7 = f32[6,224]{1,0:T(8,128)S(1)} all-reduce(f32[6,224]{1,0:T(8,128)S(1)} %get-tuple-element.19), channel_id=1, replica_groups=mesh['rec'=16,'frame'=32] {'frame'}, use_global_device_ids=true, to_apply=%region_6.0 | all-reduce | flops 1344 | bytes 10752 | tf_op jit(solution)/shard_map/pmax | solution.py:63
  185.0 4.8 fusion.9
  189.8 1.9 collective-permute-start
  191.8 24.7 %collective-permute-done = f32[6,224,256]{2,1,0:T(8,128)S(1)} collective-permute-done((f32[6,224,256]{2,1,0:T(8,128)S(1)}, f32[6,224,256]{2,1,0:T(8,128)S(1)}, u32[]{:S(2)}, u32[]{:S(2)}) %collective-permute-start) | collective-permute-done | bytes 1376288 | tf_op jit(solution)/shard_map/ppermute | solution.py:74
  216.7 8.2 %collective-permute-start.1 = (f32[6,224,256]{2,1,0:T(8,128)S(1)}, f32[6,224,256]{2,1,0:T(8,128)S(1)}, u32[]{:S(2)}, u32[]{:S(2)}) collective-permute-start(f32[6,224,256]{2,1,0:T(8,128)S(1)} %add.65), channel_id=1, source_target_pairs={{0,2},{1,3},{2,0},{3,1},{4,6},{5,7},{6,4},{7,5},{8,10},{9,11},{10,... | collective-permute-start | bytes 4128776 | tf_op jit(solution)/shard_map/ppermute | solution.py:74
  224.9 66.3 %collective-permute-done.1 = f32[6,224,256]{2,1,0:T(8,128)S(1)} collective-permute-done((f32[6,224,256]{2,1,0:T(8,128)S(1)}, f32[6,224,256]{2,1,0:T(8,128)S(1)}, u32[]{:S(2)}, u32[]{:S(2)}) %collective-permute-start.1) | collective-permute-done | bytes 1376288 | tf_op jit(solution)/shard_map/ppermute | solution.py:74
  291.4 1.9 collective-permute-start.2
  293.3 31.4 %collective-permute-done.2 = f32[6,224,256]{2,1,0:T(8,128)S(1)} collective-permute-done((f32[6,224,256]{2,1,0:T(8,128)S(1)}, f32[6,224,256]{2,1,0:T(8,128)S(1)}, u32[]{:S(2)}, u32[]{:S(2)}) %collective-permute-start.2) | collective-permute-done | bytes 1376288 | tf_op jit(solution)/shard_map/ppermute | solution.py:74
  324.9 1.9 collective-permute-start.3
  326.8 18.3 %collective-permute-done.3 = f32[6,224,256]{2,1,0:T(8,128)S(1)} collective-permute-done((f32[6,224,256]{2,1,0:T(8,128)S(1)}, f32[6,224,256]{2,1,0:T(8,128)S(1)}, u32[]{:S(2)}, u32[]{:S(2)}) %collective-permute-start.3) | collective-permute-done | bytes 1376288 | tf_op jit(solution)/shard_map/ppermute | solution.py:74
  345.3 4.4 collective-permute-start.4
  349.7 17.5 %collective-permute-done.4 = f32[6,224,256]{2,1,0:T(8,128)S(1)} collective-permute-done((f32[6,224,256]{2,1,0:T(8,128)S(1)}, f32[6,224,256]{2,1,0:T(8,128)S(1)}, u32[]{:S(2)}, u32[]{:S(2)}) %collective-permute-start.4) | collective-permute-done | bytes 1376288 | tf_op jit(solution)/shard_map/ppermute | solution.py:74
  369.0 1.6 multiply_convert_fusion.1
  370.6 2.3 multiply_convert_fusion
  372.9 2.0 copy-done.1
  374.9 2.3 convolution_bitcast_fusion.2
  381.7 5.4 convolution_bitcast_fusion
  387.1 2.4 fusion.5
  389.5 166.2 %all-reduce.6.cloned.1.call-done = f32[224,6,256]{2,0,1:T(8,128)} async-done(((f32[224,6,256]{2,0,1:T(8,128)}), f32[224,6,256]{2,0,1:T(8,128)}) %all-reduce.6.cloned.1.call-update) | async-done | bytes 1376272
  557.2 49.1 %all-reduce.7 = (f32[]{:T(128)}, bf16[32,7,256]{2,0,1:T(8,128)(2,1)S(1)}) all-reduce(f32[]{:T(128)} %get-tuple-element.18, f32[32,7,256]{2,0,1:T(8,128)S(1)} %fusion.15), channel_id=1, replica_groups=mesh['rec'=16,'frame'=32] {'rec'}, use_global_device_ids=true, to_apply=%region_10.11 | all-reduce | flops 57345 | bytes 344072 | tf_op jit(solution)/shard_map/psum | solution.py:111
  (56 shorter events, 12.0 us)
Async XLA Ops:
  7.2 102.0 %copy-start = (bf16[1,1536,256]{2,1,0:T(8,128)(2,1)S(1)}, bf16[1,1536,256]{2,1,0:T(8,128)(2,1)}, u32[]{:S(2)}) copy-start(bf16[1,1536,256]{2,1,0:T(8,128)(2,1)} %param.5) | copy-start | bytes 2359300
  7.2 97.5 %all-gather.2.cloned.1.call-start = ((), (), s32[]{:S(2)}) async-start(), calls=%async_computation | async-start | bytes 3899392 | tf_op jit(solution)/shard_map/all_gather | solution.py:51
  57.8 497.9 %all-reduce.6.cloned.1.call-start = ((), (), s32[]{:S(2)}) async-start(), calls=%async_computation.1 | async-start | bytes 2752512
  60.9 43.9 %copy-start.7 = (s32[6]{0:T(128)}, s32[6]{0:T(128)S(1)}, u32[]{:S(2)}) copy-start(s32[6]{0:T(128)S(1)} %get-tuple-element.6) | copy-start | bytes 76
  60.9 43.8 %copy-start.11 = (pred[6]{0:T(512)(128)(4,1)}, pred[6]{0:T(512)(128)(4,1)S(1)}, u32[]{:S(2)}) copy-start(pred[6]{0:T(512)(128)(4,1)S(1)} %broadcast_compare_fusion) | copy-start | bytes 22
  184.9 4.9 copy-start.3
  189.8 26.6 %collective-permute-start = (f32[6,224,256]{2,1,0:T(8,128)S(1)}, f32[6,224,256]{2,1,0:T(8,128)S(1)}, u32[]{:S(2)}, u32[]{:S(2)}) collective-permute-start(f32[6,224,256]{2,1,0:T(8,128)S(1)} %fusion.9), channel_id=1, source_target_pairs={{0,1},{1,0},{2,3},{3,2},{4,5},{5,4},{6,7},{7,6},{8,9},{9,8},{10,11... | collective-permute-start | bytes 4128776 | tf_op jit(solution)/shard_map/ppermute | solution.py:74
  216.7 74.5 %collective-permute-start.1 = (f32[6,224,256]{2,1,0:T(8,128)S(1)}, f32[6,224,256]{2,1,0:T(8,128)S(1)}, u32[]{:S(2)}, u32[]{:S(2)}) collective-permute-start(f32[6,224,256]{2,1,0:T(8,128)S(1)} %add.65), channel_id=1, source_target_pairs={{0,2},{1,3},{2,0},{3,1},{4,6},{5,7},{6,4},{7,5},{8,10},{9,11},{10,... | collective-permute-start | bytes 4128776 | tf_op jit(solution)/shard_map/ppermute | solution.py:74
  291.4 33.3 %collective-permute-start.2 = (f32[6,224,256]{2,1,0:T(8,128)S(1)}, f32[6,224,256]{2,1,0:T(8,128)S(1)}, u32[]{:S(2)}, u32[]{:S(2)}) collective-permute-start(f32[6,224,256]{2,1,0:T(8,128)S(1)} %add.66), channel_id=1, source_target_pairs={{0,4},{1,5},{2,6},{3,7},{4,0},{5,1},{6,2},{7,3},{8,12},{9,13},{10,... | collective-permute-start | bytes 4128776 | tf_op jit(solution)/shard_map/ppermute | solution.py:74
  324.9 20.2 %collective-permute-start.3 = (f32[6,224,256]{2,1,0:T(8,128)S(1)}, f32[6,224,256]{2,1,0:T(8,128)S(1)}, u32[]{:S(2)}, u32[]{:S(2)}) collective-permute-start(f32[6,224,256]{2,1,0:T(8,128)S(1)} %add.67), channel_id=1, source_target_pairs={{0,8},{1,9},{2,10},{3,11},{4,12},{5,13},{6,14},{7,15},{8,0},{9,1},... | collective-permute-start | bytes 4128776 | tf_op jit(solution)/shard_map/ppermute | solution.py:74
  345.1 25.5 %slice-start = ((s8[8257536]{0:T(1024)(128)(4,1)}), s8[4194304]{0:T(1024)(128)(4,1)S(1)}, s32[]{:S(2)}) async-start(s8[8257536]{0:T(1024)(128)(4,1)} %bitcast.46), calls=%async_computation.2 | async-start | bytes 8388608
  345.3 22.0 %collective-permute-start.4 = (f32[6,224,256]{2,1,0:T(8,128)S(1)}, f32[6,224,256]{2,1,0:T(8,128)S(1)}, u32[]{:S(2)}, u32[]{:S(2)}) collective-permute-start(f32[6,224,256]{2,1,0:T(8,128)S(1)} %add.68), channel_id=1, source_target_pairs={{0,16},{1,17},{2,18},{3,19},{4,20},{5,21},{6,22},{7,23},{8,24},{9,... | collective-permute-start | bytes 4128776 | tf_op jit(solution)/shard_map/ppermute | solution.py:74
  349.7 20.9 %slice-start.1 = ((s8[8257536]{0:T(1024)(128)(4,1)}), s8[4063232]{0:T(1024)(128)(4,1)S(1)}, s32[]{:S(2)}) async-start(s8[8257536]{0:T(1024)(128)(4,1)} %bitcast.46), calls=%async_computation.3 | async-start | bytes 8126464
  369.0 1.6 copy-start.9
  369.0 1.6 copy-start.4
  372.9 2.0 copy-start.1
  381.7 5.4 copy-start.2
  387.1 168.6 %copy-start.5 = (f32[6,7]{1,0:T(8,128)S(1)}, f32[6,7]{1,0:T(8,128)}, u32[]{:S(2)}) copy-start(f32[6,7]{1,0:T(8,128)} %get-tuple-element.21) | copy-start | bytes 508
  387.1 168.6 %copy-start.6 = (f32[6,7]{1,0:T(8,128)S(1)}, f32[6,7]{1,0:T(8,128)}, u32[]{:S(2)}) copy-start(f32[6,7]{1,0:T(8,128)} %get-tuple-element.22) | copy-start | bytes 508
  387.1 168.6 %copy-start.10 = (f32[6]{0:T(128)S(1)}, f32[6]{0:T(128)}, u32[]{:S(2)}) copy-start(f32[6]{0:T(128)} %copy-done.9) | copy-start | bytes 76
  387.1 169.6 %copy-start.8 = (s32[6]{0:T(128)S(1)}, s32[6]{0:T(128)}, u32[]{:S(2)}) copy-start(s32[6]{0:T(128)} %copy-done.7) | copy-start | bytes 76
  387.1 169.6 %copy-start.12 = (pred[6]{0:T(512)(128)(4,1)S(1)}, pred[6]{0:T(512)(128)(4,1)}, u32[]{:S(2)}) copy-start(pred[6]{0:T(512)(128)(4,1)} %copy-done.11) | copy-start | bytes 22
Sparse Core Ops, SparseCore 0:
  57.9 46.7 all-gather.1
  377.4 178.2 all-reduce.5
